TPU v7x, 256 devices: a whole 4x4x8 slice. The times are simulated.
256 devices in a mesh: vid: 64 (over z_hi, x, y), tp: 4 (over z_lo, core).
Axes of the slice: x: 4, y: 4, z: 8 (z_hi: 4, z_lo: 2; z = z_hi * 2 + z_lo), core: 2. Of those that a mesh axis runs over, the one named last changes fastest.
Arguments:
- video_x: bfloat16 [32768, 3072], P('vid', 'tp'), may hold values from -6 to 6
- audio_x: bfloat16 [4096, 3072], P('vid', 'tp'), may hold values from -6 to 6
- video_kv: bfloat16 [32768, 2, 1536], P('vid', None, 'tp'), may hold values from -500 to 500
- audio_kv: bfloat16 [4096, 2, 1536], P('vid', None, 'tp'), may hold values from -500 to 500
- wq_video: bfloat16 [3072, 1536], P(None, 'tp'), may hold values from -0.109375 to 0.109375
- wo_video: bfloat16 [1536, 3072], P('tp'), may hold values from -0.15625 to 0.15625
- wq_audio: bfloat16 [3072, 1536], P(None, 'tp'), may hold values from -0.109375 to 0.109375
- wo_audio: bfloat16 [1536, 3072], P('tp'), may hold values from -0.15625 to 0.15625
- block_list: int32 [256, 3], replicated, may hold values from 0 to 31, as said below
- video_len: int32 [1], replicated, may hold values from 31872 to 32768
- audio_len: int32 [1], replicated, may hold values from 3969 to 4096
Outputs:
- video_out: bfloat16 [32768, 3072], P('vid', 'tp')
- audio_out: bfloat16 [4096, 3072], P('vid', 'tp')
Inputs may be any that keep to these rules, and one draw needn't show every extreme that they name: `block_list`: row v holds three audio blocks, each within 2 of floor(v / 8), and floor(v / 8) itself is among them; an entry may repeat.
All inputs are finite; a program needn't handle non-finite values.
Results may differ from a plain program's by a relative error of at most 0.015.
The roundings to bfloat16 on the way count: a program that leaves them out, or rounds other values in their place, can miss the bound.
Values may be sent and summed in bfloat16 or wider, within the bound.
A program may use at most 128 MiB of HBM per device.

v0:
```python
import jax
import jax.numpy as jnp
from jax import lax
from jax.sharding import PartitionSpec as P

HDIM = 128
BLOCK = 128


NEGATIVE = -1e30


def shifted(array, axis, by):
    peers = lax.axis_size(axis)
    pairs = [(i, i + by) for i in range(peers) if 0 <= i + by < peers]
    return lax.ppermute(array, axis, pairs)


def scaled_scores(queries, key_rows):
    return jnp.einsum(
        "qhd,khd->hqk", queries, key_rows, preferred_element_type=jnp.float32
    ) * queries.shape[-1] ** (-0.5)


def window_rows(own_rows, span, mover):
    pieces = []
    for offset in range(-span, span + 1):
        if offset == 0:
            pieces.append(own_rows)
        else:
            pieces.append(mover(own_rows, -offset))
    return jnp.concatenate(pieces, axis=0)


def fold_keys(queries, query_lists, limit_audio, shard_rows, offset):
    count = shard_rows.shape[0]
    head_count = queries.shape[1]
    key_rows = shard_rows[:, 0].reshape(count, head_count, HDIM)
    values = shard_rows[:, 1].reshape(count, head_count, HDIM)
    positions = offset + jnp.arange(count, dtype=jnp.int32)
    allowed = jnp.any(query_lists[:, None, :] == (positions // BLOCK)[None, :, None], axis=-1)
    allowed = allowed & ((positions >= 0) & (positions < limit_audio))[None, :]
    scores = jnp.where(allowed[None], scaled_scores(queries, key_rows), NEGATIVE)
    row_peak = jnp.max(scores, axis=-1)
    weights = jnp.where(allowed[None], jnp.exp(scores - row_peak[:, :, None]), 0.0)
    weight_sum = jnp.sum(weights, axis=-1)
    weighted = jnp.einsum(
        "hqk,khd->qhd", weights.astype(jnp.bfloat16), values, preferred_element_type=jnp.float32
    )
    return (weight_sum, weighted)


def partial_state(query_rows, query_blocks, query_lists, key_valid, video_kv):
    key_count = video_kv.shape[0]
    head_count = query_rows.shape[1]
    allowed = jnp.any(query_lists[None, :, :] == query_blocks[:, None, None], axis=-1)
    allowed = allowed & key_valid[None, :]
    key_rows = video_kv[:, 0].reshape(key_count, head_count, HDIM)
    values = video_kv[:, 1].reshape(key_count, head_count, HDIM)
    scores = jnp.where(allowed[None], scaled_scores(query_rows, key_rows), NEGATIVE)
    row_peak = jnp.max(scores, axis=-1)
    weights = jnp.where(allowed[None], jnp.exp(scores - row_peak[:, :, None]), 0.0)
    weight_sum = jnp.sum(weights, axis=-1)
    weighted = jnp.einsum(
        "hqk,khd->qhd", weights.astype(jnp.bfloat16), values, preferred_element_type=jnp.float32
    )
    return (row_peak, weight_sum, weighted)


def per_device(
    video_x,
    audio_x,
    video_kv,
    audio_kv,
    wq_video,
    wo_video,
    wq_audio,
    wo_audio,
    block_list,
    video_len,
    audio_len,
):
    vid_rows = video_x.shape[0]
    aud_rows = audio_x.shape[0]
    local_width = wq_video.shape[1]
    head_count = local_width // HDIM
    vid_place = lax.axis_index("vid")
    first_video = vid_place * vid_rows
    first_audio = vid_place * aud_rows
    span = 3 * BLOCK // aud_rows - 1
    video_full, audio_full = (
        lax.all_gather(video_x, "tp", axis=1, tiled=True),
        lax.all_gather(audio_x, "tp", axis=1, tiled=True),
    )
    q_video = (
        jnp.dot(video_full, wq_video, preferred_element_type=jnp.float32)
        .astype(jnp.bfloat16)
        .reshape(vid_rows, head_count, HDIM)
    )
    q_audio = jnp.dot(audio_full, wq_audio, preferred_element_type=jnp.float32).astype(jnp.bfloat16)
    own_blocks = vid_rows // BLOCK
    own_lists = lax.dynamic_slice_in_dim(block_list, vid_place * own_blocks, own_blocks, 0)
    query_lists = jnp.repeat(own_lists, BLOCK, axis=0)
    limit_audio = audio_len[0]
    limit_video = video_len[0]
    reach_audio = span * aud_rows
    audio_near = window_rows(audio_kv, span, lambda piece, by: shifted(piece, "vid", by))
    weight_sum, weighted = fold_keys(
        q_video, query_lists, limit_audio, audio_near, first_audio - reach_audio
    )
    attn_video = (
        (weighted / weight_sum.T[:, :, None]).astype(jnp.bfloat16).reshape(vid_rows, local_width)
    )
    reach_video = span * vid_rows
    window = window_rows(video_kv, span, lambda piece, by: shifted(piece, "vid", by))
    pad_blocks = reach_video // BLOCK
    filler = jnp.full((pad_blocks, block_list.shape[1]), -1, jnp.int32)
    padded_lists = jnp.concatenate([filler, block_list, filler], axis=0)
    window_lists = jnp.repeat(
        lax.dynamic_slice_in_dim(
            padded_lists, vid_place * own_blocks, own_blocks + 2 * pad_blocks, 0
        ),
        BLOCK,
        axis=0,
    )
    window_count = window.shape[0]
    window_positions = first_video - reach_video + jnp.arange(window_count, dtype=jnp.int32)
    query_blocks = (first_audio + jnp.arange(aud_rows, dtype=jnp.int32)) // BLOCK
    row_peak, audio_sum, audio_weighted = partial_state(
        q_audio.reshape(aud_rows, head_count, HDIM),
        query_blocks,
        window_lists,
        window_positions < limit_video,
        window,
    )
    attn_audio = (
        (audio_weighted / audio_sum.T[:, :, None])
        .astype(jnp.bfloat16)
        .reshape(aud_rows, local_width)
    )
    video_part = jnp.dot(attn_video, wo_video, preferred_element_type=jnp.float32)
    audio_part = jnp.dot(attn_audio, wo_audio, preferred_element_type=jnp.float32)
    video_out, audio_out = (
        lax.psum_scatter(
            video_part.astype(jnp.bfloat16), "tp", scatter_dimension=1, tiled=True
        ).astype(jnp.float32),
        lax.psum_scatter(
            audio_part.astype(jnp.bfloat16), "tp", scatter_dimension=1, tiled=True
        ).astype(jnp.float32),
    )
    return (video_out.astype(jnp.bfloat16), audio_out.astype(jnp.bfloat16))


def solution(mesh):
    in_specs = (
        P("vid", "tp"),
        P("vid", "tp"),
        P("vid", None, "tp"),
        P("vid", None, "tp"),
        P(None, "tp"),
        P("tp", None),
        P(None, "tp"),
        P("tp", None),
        P(),
        P(),
        P(),
    )
    out_specs = (P("vid", "tp"), P("vid", "tp"))
    return jax.shard_map(
        per_device, mesh=mesh, in_specs=in_specs, out_specs=out_specs, check_vma=False
    )
```

profile of v0, /device:TPU:1, one launch (start us, length us, event | category | flops | bytes accessed | tf_op | source)
XLA Modules:
  0.0 560.2 jit_solution(9463965026226202909)
XLA Ops:
  7.2 3.2 copy.44
  10.4 5.8 %collective-permute-start.10 = (bf16[512,2,384]{0,2,1:T(8,128)(2,1)}, bf16[512,2,384]{0,2,1:T(8,128)(2,1)}, u32[]{:S(2)}, u32[]{:S(2)}) collective-permute-start(bf16[512,2,384]{0,2,1:T(8,128)(2,1)} %copy.44), channel_id=1, source_target_pairs={{0,20},{4,24},{8,28},{12,32},{16,36},{20,40},{24,44},{28,48},{32,5... | collective-permute-start | bytes 2359304 | tf_op jit(solution)/shard_map/ppermute | solution.py:16
  16.3 4.0 collective-permute-start.11
  20.3 4.0 collective-permute-start.12
  24.2 3.6 collective-permute-start.13
  27.8 3.2 collective-permute-start
  32.7 9.0 %all_gather.7 = bf16[64,3072]{1,0:T(8,128)(2,1)S(1)} all-gather(bf16[64,768]{1,0:T(8,128)(2,1)} %param.12), channel_id=1, replica_groups=mesh['vid'=64,'tp'=4] {'tp'}, dimensions={1}, use_global_device_ids=true | all-gather | bytes 491520 | tf_op jit(solution)/shard_map/all_gather | solution.py:93
  45.0 2.3 fusion.32
  48.9 2.0 collective-permute-done
  50.9 3.1 collective-permute-start.1
  54.1 1.5 collective-permute-done.1
  55.6 38.8 %collective-permute-start.2 = (bf16[64,2,384]{2,1,0:T(2,128)(2,1)S(1)}, bf16[64,2,384]{2,1,0:T(2,128)(2,1)S(1)}, u32[]{:S(2)}, u32[]{:S(2)}) collective-permute-start(bf16[64,2,384]{2,1,0:T(2,128)(2,1)S(1)} %copy-done.5), channel_id=1, source_target_pairs={{0,12},{4,16},{8,20},{12,24},{16,28},{20,32},{24,36},{28,40},{32,4... | collective-permute-start | bytes 294920 | tf_op jit(solution)/shard_map/ppermute | solution.py:16
  94.5 1.5 collective-permute-done.2
  96.0 1.3 collective-permute-start.3
  97.4 1.5 collective-permute-done.3
  98.9 15.7 %collective-permute-start.4 = (bf16[64,2,384]{2,1,0:T(2,128)(2,1)S(1)}, bf16[64,2,384]{2,1,0:T(2,128)(2,1)S(1)}, u32[]{:S(2)}, u32[]{:S(2)}) collective-permute-start(bf16[64,2,384]{2,1,0:T(2,128)(2,1)S(1)} %copy-done.5), channel_id=1, source_target_pairs={{0,4},{4,8},{8,12},{12,16},{16,20},{20,24},{24,28},{28,32},{32,36}... | collective-permute-start | bytes 294920 | tf_op jit(solution)/shard_map/ppermute | solution.py:16
  114.8 1.5 collective-permute-done.4
  116.3 1.3 collective-permute-start.5
  117.8 4.2 collective-permute-done.5
  122.0 1.3 collective-permute-start.6
  123.4 11.2 %collective-permute-done.6 = bf16[64,2,384]{2,1,0:T(2,128)(2,1)S(1)} collective-permute-done((bf16[64,2,384]{2,1,0:T(2,128)(2,1)S(1)}, bf16[64,2,384]{2,1,0:T(2,128)(2,1)S(1)}, u32[]{:S(2)}, u32[]{:S(2)}) %collective-permute-start.6) | collective-permute-done | bytes 98336 | tf_op jit(solution)/shard_map/ppermute | solution.py:16
  134.6 1.3 collective-permute-start.7
  135.9 23.8 %collective-permute-done.7 = bf16[64,2,384]{2,1,0:T(2,128)(2,1)S(1)} collective-permute-done((bf16[64,2,384]{2,1,0:T(2,128)(2,1)S(1)}, bf16[64,2,384]{2,1,0:T(2,128)(2,1)S(1)}, u32[]{:S(2)}, u32[]{:S(2)}) %collective-permute-start.7) | collective-permute-done | bytes 98336 | tf_op jit(solution)/shard_map/ppermute | solution.py:16
  159.8 1.3 collective-permute-start.8
  161.2 10.6 %collective-permute-done.8 = bf16[64,2,384]{2,1,0:T(2,128)(2,1)S(1)} collective-permute-done((bf16[64,2,384]{2,1,0:T(2,128)(2,1)S(1)}, bf16[64,2,384]{2,1,0:T(2,128)(2,1)S(1)}, u32[]{:S(2)}, u32[]{:S(2)}) %collective-permute-start.8) | collective-permute-done | bytes 98336 | tf_op jit(solution)/shard_map/ppermute | solution.py:16
  171.8 1.3 collective-permute-start.9
  173.2 5.2 collective-permute-done.9
  178.3 8.9 %collective-permute-start.14 = (bf16[512,2,384]{0,2,1:T(8,128)(2,1)}, bf16[512,2,384]{0,2,1:T(8,128)(2,1)}, u32[]{:S(2)}, u32[]{:S(2)}) collective-permute-start(bf16[512,2,384]{0,2,1:T(8,128)(2,1)} %copy.44), channel_id=1, source_target_pairs={{0,4},{4,8},{8,12},{12,16},{16,20},{20,24},{24,28},{28,32},{32,36}... | collective-permute-start | bytes 2359304 | tf_op jit(solution)/shard_map/ppermute | solution.py:16
  187.4 2.4 fusion.53
  189.7 4.5 copy.40
  194.2 3.1 copy.39
  197.3 1.3 collective-permute-start.15
  199.8 1.3 collective-permute-start.16
  202.3 1.3 collective-permute-start.17
  204.8 1.3 collective-permute-start.18
  207.3 1.3 collective-permute-start.19
  211.1 15.9 %collective-permute-done.16 = bf16[512,2,384]{0,2,1:T(8,128)(2,1)S(1)} collective-permute-done((bf16[512,2,384]{0,2,1:T(8,128)(2,1)}, bf16[512,2,384]{0,2,1:T(8,128)(2,1)S(1)}, u32[]{:S(2)}, u32[]{:S(2)}) %collective-permute-start.16) | collective-permute-done | bytes 786464 | tf_op jit(solution)/shard_map/ppermute | solution.py:16
  227.0 15.1 %collective-permute-done.17 = bf16[512,2,384]{0,2,1:T(8,128)(2,1)S(1)} collective-permute-done((bf16[512,2,384]{0,2,1:T(8,128)(2,1)}, bf16[512,2,384]{0,2,1:T(8,128)(2,1)S(1)}, u32[]{:S(2)}, u32[]{:S(2)}) %collective-permute-start.17) | collective-permute-done | bytes 786464 | tf_op jit(solution)/shard_map/ppermute | solution.py:16
  242.2 109.4 %collective-permute-done.18 = bf16[512,2,384]{0,2,1:T(8,128)(2,1)S(1)} collective-permute-done((bf16[512,2,384]{0,2,1:T(8,128)(2,1)}, bf16[512,2,384]{0,2,1:T(8,128)(2,1)S(1)}, u32[]{:S(2)}, u32[]{:S(2)}) %collective-permute-start.18) | collective-permute-done | bytes 786464 | tf_op jit(solution)/shard_map/ppermute | solution.py:16
  353.9 1.3 fusion.55
  355.3 1.6 fusion.33
  356.9 1.3 convolution_convert_fusion.1
  358.5 4.8 convolution_convert_fusion.2
  363.3 5.0 fusion.54
  368.3 2.1 fusion.20
  370.4 3.5 convolution_convert_fusion
  373.9 136.8 %reduce-scatter.5.cloned.1.call-done = bf16[64,768]{1,0:T(8,128)(2,1)} async-done(((bf16[64,3072]{1,0:T(8,128)(2,1)}), bf16[64,768]{1,0:T(8,128)(2,1)}) %reduce-scatter.5.cloned.1.call-update) | async-done | bytes 98320 | tf_op jit(solution)/shard_map/reduce_scatter | solution.py:147
  510.7 42.9 %reduce-scatter.3.cloned.1.call-done = bf16[512,768]{1,0:T(8,128)(2,1)} async-done(((bf16[512,3072]{1,0:T(8,128)(2,1)}), bf16[512,768]{1,0:T(8,128)(2,1)}) %reduce-scatter.3.cloned.1.call-update) | async-done | bytes 786448 | tf_op jit(solution)/shard_map/reduce_scatter | solution.py:144
  (65 shorter events, 16.1 us)
Async XLA Ops:
  7.2 363.2 %copy-start = (bf16[384,3072]{1,0:T(8,128)(2,1)S(1)}, bf16[384,3072]{1,0:T(8,128)(2,1)}, u32[]{:S(2)}) copy-start(bf16[384,3072]{1,0:T(8,128)(2,1)} %param.16) | copy-start | bytes 7077892
  7.2 351.3 %all-gather.2.cloned.1.call-start = ((), (), s32[]{:S(2)}) async-start(), calls=%async_computation.2 | async-start | bytes 3932160 | tf_op jit(solution)/shard_map/all_gather | solution.py:92
  10.4 186.9 %collective-permute-start.10 = (bf16[512,2,384]{0,2,1:T(8,128)(2,1)}, bf16[512,2,384]{0,2,1:T(8,128)(2,1)}, u32[]{:S(2)}, u32[]{:S(2)}) collective-permute-start(bf16[512,2,384]{0,2,1:T(8,128)(2,1)} %copy.44), channel_id=1, source_target_pairs={{0,20},{4,24},{8,28},{12,32},{16,36},{20,40},{24,44},{28,48},{32,5... | collective-permute-start | bytes 2359304 | tf_op jit(solution)/shard_map/ppermute | solution.py:16
  16.3 183.6 %collective-permute-start.11 = (bf16[512,2,384]{0,2,1:T(8,128)(2,1)}, bf16[512,2,384]{0,2,1:T(8,128)(2,1)}, u32[]{:S(2)}, u32[]{:S(2)}) collective-permute-start(bf16[512,2,384]{0,2,1:T(8,128)(2,1)} %copy.44), channel_id=1, source_target_pairs={{0,16},{4,20},{8,24},{12,28},{16,32},{20,36},{24,40},{28,44},{32,4... | collective-permute-start | bytes 2359304 | tf_op jit(solution)/shard_map/ppermute | solution.py:16
  20.3 182.0 %collective-permute-start.12 = (bf16[512,2,384]{0,2,1:T(8,128)(2,1)}, bf16[512,2,384]{0,2,1:T(8,128)(2,1)}, u32[]{:S(2)}, u32[]{:S(2)}) collective-permute-start(bf16[512,2,384]{0,2,1:T(8,128)(2,1)} %copy.44), channel_id=1, source_target_pairs={{0,12},{4,16},{8,20},{12,24},{16,28},{20,32},{24,36},{28,40},{32,4... | collective-permute-start | bytes 2359304 | tf_op jit(solution)/shard_map/ppermute | solution.py:16
  24.2 180.6 %collective-permute-start.13 = (bf16[512,2,384]{0,2,1:T(8,128)(2,1)}, bf16[512,2,384]{0,2,1:T(8,128)(2,1)}, u32[]{:S(2)}, u32[]{:S(2)}) collective-permute-start(bf16[512,2,384]{0,2,1:T(8,128)(2,1)} %copy.44), channel_id=1, source_target_pairs={{0,8},{4,12},{8,16},{12,20},{16,24},{20,28},{24,32},{28,36},{32,40... | collective-permute-start | bytes 2359304 | tf_op jit(solution)/shard_map/ppermute | solution.py:16
  27.8 23.0 %collective-permute-start = (bf16[64,2,384]{2,1,0:T(2,128)(2,1)}, bf16[64,2,384]{2,1,0:T(2,128)(2,1)S(1)}, u32[]{:S(2)}, u32[]{:S(2)}) collective-permute-start(bf16[64,2,384]{2,1,0:T(2,128)(2,1)} %param.14), channel_id=1, source_target_pairs={{0,20},{4,24},{8,28},{12,32},{16,36},{20,40},{24,44},{28,48},{32,5... | collective-permute-start | bytes 294920 | tf_op jit(solution)/shard_map/ppermute | solution.py:16
  31.0 19.9 %copy-start.5 = (bf16[64,2,384]{2,1,0:T(2,128)(2,1)S(1)}, bf16[64,2,384]{2,1,0:T(2,128)(2,1)}, u32[]{:S(2)}) copy-start(bf16[64,2,384]{2,1,0:T(2,128)(2,1)} %param.14) | copy-start | bytes 294916
  31.0 479.7 %reduce-scatter.5.cloned.1.call-start = ((), (), s32[]{:S(2)}) async-start(), calls=%async_computation.4 | async-start | bytes 491520 | tf_op jit(solution)/shard_map/reduce_scatter | solution.py:147
  50.9 4.7 collective-permute-start.1
  55.6 40.4 %collective-permute-start.2 = (bf16[64,2,384]{2,1,0:T(2,128)(2,1)S(1)}, bf16[64,2,384]{2,1,0:T(2,128)(2,1)S(1)}, u32[]{:S(2)}, u32[]{:S(2)}) collective-permute-start(bf16[64,2,384]{2,1,0:T(2,128)(2,1)S(1)} %copy-done.5), channel_id=1, source_target_pairs={{0,12},{4,16},{8,20},{12,24},{16,28},{20,32},{24,36},{28,40},{32,4... | collective-permute-start | bytes 294920 | tf_op jit(solution)/shard_map/ppermute | solution.py:16
  96.0 2.9 collective-permute-start.3
  98.9 17.4 %collective-permute-start.4 = (bf16[64,2,384]{2,1,0:T(2,128)(2,1)S(1)}, bf16[64,2,384]{2,1,0:T(2,128)(2,1)S(1)}, u32[]{:S(2)}, u32[]{:S(2)}) collective-permute-start(bf16[64,2,384]{2,1,0:T(2,128)(2,1)S(1)} %copy-done.5), channel_id=1, source_target_pairs={{0,4},{4,8},{8,12},{12,16},{16,20},{20,24},{24,28},{28,32},{32,36}... | collective-permute-start | bytes 294920 | tf_op jit(solution)/shard_map/ppermute | solution.py:16
  116.3 5.7 %collective-permute-start.5 = (bf16[64,2,384]{2,1,0:T(2,128)(2,1)S(1)}, bf16[64,2,384]{2,1,0:T(2,128)(2,1)S(1)}, u32[]{:S(2)}, u32[]{:S(2)}) collective-permute-start(bf16[64,2,384]{2,1,0:T(2,128)(2,1)S(1)} %copy-done.5), channel_id=1, source_target_pairs={{4,0},{8,4},{12,8},{16,12},{20,16},{24,20},{28,24},{32,28},{36,32}... | collective-permute-start | bytes 294920 | tf_op jit(solution)/shard_map/ppermute | solution.py:16
  122.0 12.5 %collective-permute-start.6 = (bf16[64,2,384]{2,1,0:T(2,128)(2,1)S(1)}, bf16[64,2,384]{2,1,0:T(2,128)(2,1)S(1)}, u32[]{:S(2)}, u32[]{:S(2)}) collective-permute-start(bf16[64,2,384]{2,1,0:T(2,128)(2,1)S(1)} %copy-done.5), channel_id=1, source_target_pairs={{8,0},{12,4},{16,8},{20,12},{24,16},{28,20},{32,24},{36,28},{40,32... | collective-permute-start | bytes 294920 | tf_op jit(solution)/shard_map/ppermute | solution.py:16
  134.6 25.2 %collective-permute-start.7 = (bf16[64,2,384]{2,1,0:T(2,128)(2,1)S(1)}, bf16[64,2,384]{2,1,0:T(2,128)(2,1)S(1)}, u32[]{:S(2)}, u32[]{:S(2)}) collective-permute-start(bf16[64,2,384]{2,1,0:T(2,128)(2,1)S(1)} %copy-done.5), channel_id=1, source_target_pairs={{12,0},{16,4},{20,8},{24,12},{28,16},{32,20},{36,24},{40,28},{44,3... | collective-permute-start | bytes 294920 | tf_op jit(solution)/shard_map/ppermute | solution.py:16
  159.8 12.0 %collective-permute-start.8 = (bf16[64,2,384]{2,1,0:T(2,128)(2,1)S(1)}, bf16[64,2,384]{2,1,0:T(2,128)(2,1)S(1)}, u32[]{:S(2)}, u32[]{:S(2)}) collective-permute-start(bf16[64,2,384]{2,1,0:T(2,128)(2,1)S(1)} %copy-done.5), channel_id=1, source_target_pairs={{16,0},{20,4},{24,8},{28,12},{32,16},{36,20},{40,24},{44,28},{48,3... | collective-permute-start | bytes 294920 | tf_op jit(solution)/shard_map/ppermute | solution.py:16
  171.8 6.5 %collective-permute-start.9 = (bf16[64,2,384]{2,1,0:T(2,128)(2,1)S(1)}, bf16[64,2,384]{2,1,0:T(2,128)(2,1)S(1)}, u32[]{:S(2)}, u32[]{:S(2)}) collective-permute-start(bf16[64,2,384]{2,1,0:T(2,128)(2,1)S(1)} %copy-done.5), channel_id=1, source_target_pairs={{20,0},{24,4},{28,8},{32,12},{36,16},{40,20},{44,24},{48,28},{52,3... | collective-permute-start | bytes 294920 | tf_op jit(solution)/shard_map/ppermute | solution.py:16
  178.3 29.0 %collective-permute-start.14 = (bf16[512,2,384]{0,2,1:T(8,128)(2,1)}, bf16[512,2,384]{0,2,1:T(8,128)(2,1)}, u32[]{:S(2)}, u32[]{:S(2)}) collective-permute-start(bf16[512,2,384]{0,2,1:T(8,128)(2,1)} %copy.44), channel_id=1, source_target_pairs={{0,4},{4,8},{8,12},{12,16},{16,20},{20,24},{24,28},{28,32},{32,36}... | collective-permute-start | bytes 2359304 | tf_op jit(solution)/shard_map/ppermute | solution.py:16
  197.3 13.7 %collective-permute-start.15 = (bf16[512,2,384]{0,2,1:T(8,128)(2,1)}, bf16[512,2,384]{0,2,1:T(8,128)(2,1)S(1)}, u32[]{:S(2)}, u32[]{:S(2)}) collective-permute-start(bf16[512,2,384]{0,2,1:T(8,128)(2,1)} %copy.44), channel_id=1, source_target_pairs={{4,0},{8,4},{12,8},{16,12},{20,16},{24,20},{28,24},{32,28},{36,32}... | collective-permute-start | bytes 2359304 | tf_op jit(solution)/shard_map/ppermute | solution.py:16
  199.8 27.1 %collective-permute-start.16 = (bf16[512,2,384]{0,2,1:T(8,128)(2,1)}, bf16[512,2,384]{0,2,1:T(8,128)(2,1)S(1)}, u32[]{:S(2)}, u32[]{:S(2)}) collective-permute-start(bf16[512,2,384]{0,2,1:T(8,128)(2,1)} %copy.44), channel_id=1, source_target_pairs={{8,0},{12,4},{16,8},{20,12},{24,16},{28,20},{32,24},{36,28},{40,32... | collective-permute-start | bytes 2359304 | tf_op jit(solution)/shard_map/ppermute | solution.py:16
  202.3 39.8 %collective-permute-start.17 = (bf16[512,2,384]{0,2,1:T(8,128)(2,1)}, bf16[512,2,384]{0,2,1:T(8,128)(2,1)S(1)}, u32[]{:S(2)}, u32[]{:S(2)}) collective-permute-start(bf16[512,2,384]{0,2,1:T(8,128)(2,1)} %copy.44), channel_id=1, source_target_pairs={{12,0},{16,4},{20,8},{24,12},{28,16},{32,20},{36,24},{40,28},{44,3... | collective-permute-start | bytes 2359304 | tf_op jit(solution)/shard_map/ppermute | solution.py:16
  204.8 146.7 %collective-permute-start.18 = (bf16[512,2,384]{0,2,1:T(8,128)(2,1)}, bf16[512,2,384]{0,2,1:T(8,128)(2,1)S(1)}, u32[]{:S(2)}, u32[]{:S(2)}) collective-permute-start(bf16[512,2,384]{0,2,1:T(8,128)(2,1)} %copy.44), channel_id=1, source_target_pairs={{16,0},{20,4},{24,8},{28,12},{32,16},{36,20},{40,24},{44,28},{48,3... | collective-permute-start | bytes 2359304 | tf_op jit(solution)/shard_map/ppermute | solution.py:16
  207.3 144.3 %collective-permute-start.19 = (bf16[512,2,384]{0,2,1:T(8,128)(2,1)}, bf16[512,2,384]{0,2,1:T(8,128)(2,1)S(1)}, u32[]{:S(2)}, u32[]{:S(2)}) collective-permute-start(bf16[512,2,384]{0,2,1:T(8,128)(2,1)} %copy.44), channel_id=1, source_target_pairs={{20,0},{24,4},{28,8},{32,12},{36,16},{40,20},{44,24},{48,28},{52,3... | collective-permute-start | bytes 2359304 | tf_op jit(solution)/shard_map/ppermute | solution.py:16
  351.7 1.0 copy-start.1
  355.3 1.7 copy-start.2
  358.3 5.1 copy-start.4
  358.3 195.4 %reduce-scatter.3.cloned.1.call-start = ((), (), s32[]{:S(2)}) async-start(), calls=%async_computation.3 | async-start | bytes 3932160 | tf_op jit(solution)/shard_map/reduce_scatter | solution.py:144
  363.3 5.0 copy-start.3
Sparse Core Ops, SparseCore 0:
  31.1 42.9 all-gather.1
  358.4 152.3 reduce-scatter.4
  514.0 39.5 reduce-scatter.2
where the time goes:
time: 561 us; the launch traced here: 560 us
  waiting for transfers between devices  383 us (68%)
  starting transfers between devices  102 us (18%)
  local copies, waits for them, and re-layouts  23.6 us (4%)
  matrix products  21.8 us (4%)
  between operations  15.5 us (3%)
  blocking collectives  9.01 us (2%)
    ppermute x20, waiting for transfers between devices, shifted(): return lax.ppermute(array, axis, pairs)  204 us
    reduce_scatter x1, waiting for transfers between devices, per_device(): lax.psum_scatter(audio_part.astype(jnp.bfloat16), 'tp', scatter_dimension...  137 us
    ppermute x20, starting transfers between devices, shifted(): return lax.ppermute(array, axis, pairs)  101 us
    reduce_scatter x1, waiting for transfers between devices, per_device(): lax.psum_scatter(video_part.astype(jnp.bfloat16), 'tp', scatter_dimension...  42.9 us
    unnamed x37, local copies, waits for them, and re-layouts  12.1 us
  transfers between devices with their start and end apart: 23, of which 15 were waited for; matrix products, arithmetic and copies ran while one was open for 8% of the time, Pallas kernels for 0%

commit v1 on v0

v1 whole, which is shorter than its diff:
```python
import math

import jax
import jax.numpy as jnp
from jax import lax
from jax.experimental import pallas as pl
from jax.experimental.pallas import tpu as pltpu
from jax.sharding import PartitionSpec as P

MESH = pl.DeviceIdType.MESH
HDIM = 128
BLOCK = 128
NEG = -1e30
BF = jnp.bfloat16
F32 = jnp.float32
SCALE = HDIM ** (-0.5) * math.log2(math.e)

COPIES = 64


def dot(a, b):
    return jnp.dot(a, b, preferred_element_type=F32)


def dot_t(a, b):
    return lax.dot_general(a, b, (((1,), (1,)), ((), ())), preferred_element_type=F32)


def split3(value):
    hi = value.astype(BF).astype(F32)
    rest = value - hi
    mid = rest.astype(BF).astype(F32)
    return hi, mid, rest - mid


def pack_stats(stats, rows):
    lane = lax.broadcasted_iota(jnp.int32, (rows, 128), 1)
    out = jnp.zeros((rows, 128), F32)
    at = 0
    for value in stats:
        for part in split3(value):
            out = jnp.where(lane == at, part, out)
            at += 1
    return out.astype(BF)


def unpack_stat(tile, at):
    return tile[:, at : at + 1] + tile[:, at + 1 : at + 2] + tile[:, at + 2 : at + 3]


def merge(packed, heads):
    peaks, sums, accs = [], [], []
    for hh in range(heads):
        ms = [unpack_stat(tile, hh * 6) for tile, _ in packed]
        ls = [unpack_stat(tile, hh * 6 + 3) for tile, _ in packed]
        peak = ms[0]
        for m in ms[1:]:
            peak = jnp.maximum(peak, m)
        total, acc = 0.0, 0.0
        for m, l, (_, a) in zip(ms, ls, packed):
            w = jnp.exp2(m - peak)
            total = total + w * l
            acc = acc + w * a[hh]
        peaks.append(peak)
        sums.append(total)
        accs.append(acc)
    return peaks, sums, accs


def kernel(
    x_hbm, xa_hbm, kv_hbm, akv_hbm, wq_hbm, wo_hbm, wqa_hbm, woa_hbm, bl, vlen, alen,
    outv, outa,
    X, XA, kvraw, VK, akraw, KW, QW, WQ, WQA, WOC, WOAC, ATT, ATTA,
    SBA, RBA, OWNA, PS, PR, SX, RX, KS, lsem, ssem, rsem,
):
    width = WQ.shape[1]
    heads = width // HDIM
    feat = x_hbm.shape[1]
    arows = xa_hbm.shape[0]
    v = lax.axis_index("vid")
    t = lax.axis_index("tp")
    y = lax.rem(v, 4)
    row = lax.div(v, 4)
    h = lax.div(y, 2)
    c = lax.rem(t, 2)
    zl = lax.div(t, 2)
    tz = lax.rem(t + 2, 4)
    tc = t + 1 - 2 * c
    y1, y2, y3 = y + 1 - 2 * lax.rem(y, 2), lax.rem(y + 2, 4), 3 - y
    nz, nc = (v, tz), (v, tc)
    vo = lax.rem(v + 64 + 16 * (2 * zl - 1), 64)
    td = lax.rem(tc + 2, 4)
    no, nd = (vo, tz), (vo, td)
    plane = lax.div(v, 16) * 16
    x = lax.div(v - plane, 4)
    nxr, nxl = (plane + lax.rem(v - plane + 4, 16), t), (plane + lax.rem(v - plane + 12, 16), t)
    ny1, ny2, ny3 = (row * 4 + y1, t), (row * 4 + y2, t), (row * 4 + y3, t)
    nup, ndn = (lax.rem(v + 4, 64), t), (lax.rem(v + 60, 64), t)

    local = {}

    def load(name, i, src, dst):
        local[name] = pltpu.make_async_copy(src, dst, lsem.at[i])
        local[name].start()

    def cols(i, n):
        return pl.ds(pl.multiple_of(i * n, n), n)

    def shard(i):
        return pl.ds(pl.multiple_of(i * arows, arows), arows)

    load("ak", 0, akv_hbm, akraw)
    load("xa", 1, xa_hbm, XA.at[:, cols(t, feat)])
    load("x", 2, x_hbm, X.at[:, cols(t, feat)])
    load("wqa", 3, wqa_hbm, WQA)
    load("wq", 4, wq_hbm, WQ)
    load("kv", 5, kv_hbm, kvraw)
    orow = pl.ds(pl.multiple_of(c * width, width), width)
    load("wo", 6, wo_hbm.at[:, cols(t, feat)], WOC.at[cols(t, width), :])
    load("wa0", 7, woa_hbm.at[:, cols(zl * 2 + c, feat)], WOAC.at[orow, pl.ds(0, feat)])
    load("wa1", 8, woa_hbm.at[:, cols((1 - zl) * 2 + c, feat)], WOAC.at[orow, pl.ds(feat, feat)])

    barrier = pltpu.get_barrier_semaphore()
    for peer in (nz, nc, ny1, ny2, ny3, nup, ndn, no, nd, nxr, nxl):
        pl.semaphore_signal(barrier, inc=1, device_id=peer, device_id_type=MESH)
    own, lower, upper = 4 + y, y, 8 + y
    sel = y + 8 * (1 - h)
    local["ak"].wait()
    KW[own] = akraw[...].reshape(arows, 2 * width)
    pl.semaphore_wait(barrier, 11)

    sent = {}

    def send(name, src, dst, peer):
        i = len(sent)
        sent[name] = pltpu.make_async_remote_copy(
            src_ref=src, dst_ref=dst, send_sem=ssem.at[i], recv_sem=rsem.at[i],
            device_id=peer, device_id_type=MESH,
        )
        sent[name].start()

    def got(*names):
        for name in names:
            sent[name].wait_recv()

    tcols, zcols = cols(t, feat), cols(tz, feat)

    def send_x(i):
        rows = pl.ds(i * BLOCK, BLOCK)
        send(f"xz{i}", x_hbm.at[rows, :], X.at[rows, tcols], nz)

    def spread_x(p, buf):
        send(p + "up", buf.at[own], buf.at[lower], nup)
        send(p + "dn", buf.at[own], buf.at[upper], ndn)

    def spread_y(p, buf):
        send(p + "y1", buf.at[own], buf.at[own], ny1)
        send(p + "y2", buf.at[own], buf.at[own], ny2)
        send(p + "y3", buf.at[own], buf.at[own], ny3)

    def spread_on(p, buf):
        got(p + "up", p + "dn")
        send(p + "f1a", buf.at[lower], buf.at[lower], ny1)
        send(p + "f1b", buf.at[upper], buf.at[upper], ny1)
        send(p + "f2", buf.at[sel], buf.at[sel], ny2)
        send(p + "f3", buf.at[sel], buf.at[sel], ny3)

    def spread_end(p):
        got(*(p + s for s in ("y1", "y2", "y3", "f1a", "f1b", "f2", "f3")))

    spread_x("k", KW)
    send("xaz", xa_hbm, XA.at[:, tcols], nz)
    send("xac", xa_hbm, XA.at[:, tcols], nc)
    send_x(0)
    spread_y("k", KW)
    send("xc", x_hbm, X.at[:, tcols], nc)

    send("woc", wo_hbm.at[:, cols(tc, feat)], WOC.at[cols(t, width), :], nc)
    part4 = width // 4

    def quarter(to, at):
        return pl.ds(pl.multiple_of(to * width + at * part4, part4), part4)

    for name, to, peer in (("woo", tz, no), ("wod", td, nd)):
        send(name, wo_hbm.at[pl.ds(pl.multiple_of(x * part4, part4), part4), cols(to, feat)],
             WOC.at[quarter(t, x), :], peer)

    def wring1():
        got("woo", "wod")
        for tag, to in (("a", tz), ("b", td)):
            rows = quarter(to, x)
            send("wr" + tag, WOC.at[rows, :], WOC.at[rows, :], nxr)
            send("wl" + tag, WOC.at[rows, :], WOC.at[rows, :], nxl)

    def wring2():
        got("wra", "wrb", "wla", "wlb")
        rows = quarter(tz, lax.rem(x + 3, 4))
        send("wr2", WOC.at[rows, :], WOC.at[rows, :], nxr)
        rows = quarter(td, lax.rem(x + 1, 4))
        send("wl2", WOC.at[rows, :], WOC.at[rows, :], nxl)

    send("wa0", woa_hbm.at[:, cols(zl * 2 + 1 - c, feat)], WOAC.at[orow, pl.ds(0, feat)], nc)
    send("wa1", woa_hbm.at[:, cols((1 - zl) * 2 + 1 - c, feat)], WOAC.at[orow, pl.ds(feat, feat)], nc)

    local["kv"].wait()
    VK[...] = kvraw[...].reshape(kvraw.shape[0], 2 * width)

    def v1(i):
        rows = pl.ds(i * BLOCK, BLOCK)
        got(f"xz{i}")
        send(f"xf{i}", X.at[rows, zcols], X.at[rows, zcols], nc)

    lane = lax.broadcasted_iota(jnp.int32, (1, BLOCK), 1)

    def v2(i):
        rows = pl.ds(i * BLOCK, BLOCK)
        vb = v * 4 + i
        entries = [bl[k, vb] for k in range(3)]
        doubles = [None, entries[1] == entries[0],
                   (entries[2] == entries[0]) | (entries[2] == entries[1])]
        bias = []
        for k in range(3):
            slot = jnp.clip(entries[k] - 2 * row + 2, 0, 5)
            for half in range(2):
                KS[pl.ds(k * BLOCK + half * arows, arows), :] = KW[slot * 2 + half]
            limit = alen[0] - entries[k] * BLOCK
            if k:
                limit = jnp.where(doubles[k], 0, limit)
            bias.append(jnp.where(lane < limit, 0.0, NEG))
        bias = jnp.concatenate(bias, axis=1)
        got(f"xf{i}")
        q = dot(X[rows, :], WQ[...]).astype(BF)
        for hh in range(heads):
            hc = pl.ds(hh * HDIM, HDIM)
            s = dot_t(q[:, hh * HDIM : (hh + 1) * HDIM], KS[:, hc]) * SCALE + bias
            e = jnp.exp2(s - jnp.max(s, axis=1, keepdims=True))
            total = jnp.sum(e, axis=1, keepdims=True)
            acc = dot(e.astype(BF), KS[:, pl.ds(width + hh * HDIM, HDIM)])
            ATT[rows, pl.ds(pl.multiple_of(t * width + hh * HDIM, HDIM), HDIM)] = (
                acc / total
            ).astype(BF)
        mine = cols(t, width)
        send(f"az{i}", ATT.at[rows, mine], ATT.at[rows, mine], nz)
        send(f"ac{i}", ATT.at[rows, mine], ATT.at[rows, mine], nc)

    def v3(i):
        rows = pl.ds(i * BLOCK, BLOCK)
        other = cols(tz, width)
        got(f"az{i}")
        send(f"af{i}", ATT.at[rows, other], ATT.at[rows, other], nc)

    def v4(i):
        rows = pl.ds(i * BLOCK, BLOCK)
        got(f"ac{i}", f"af{i}")
        outv[rows, :] = dot(ATT[rows, :], WOC[...]).astype(BF)

    def a4():
        base = v * 4

        def block(j, _):
            g = h + j
            blk = 2 * row - 2 + g
            bias = []
            for k in range(4):
                vb = base + k
                linked = (bl[0, vb] == blk) | (bl[1, vb] == blk) | (bl[2, vb] == blk)
                limit = jnp.where(linked, vlen[0] - vb * BLOCK, 0)
                bias.append(jnp.where(lane < limit, 0.0, NEG))
            bias = jnp.concatenate(bias, axis=1)
            rows = pl.ds(pl.multiple_of(g * BLOCK, BLOCK), BLOCK)
            stats = []
            qs = jnp.concatenate([QW[2 * g], QW[2 * g + 1]], axis=0)
            for hh in range(heads):
                hc = pl.ds(hh * HDIM, HDIM)
                s = dot_t(qs[:, hh * HDIM : (hh + 1) * HDIM], VK[:, hc]) * SCALE + bias
                m = jnp.max(s, axis=1, keepdims=True)
                e = jnp.exp2(s - m)
                stats += [m, jnp.sum(e, axis=1, keepdims=True)]
                PS[rows, hc] = dot(e.astype(BF), VK[:, pl.ds(width + hh * HDIM, HDIM)]).astype(BF)
            PS[rows, pl.ds(width, 128)] = pack_stats(stats, BLOCK)
            return 0

        lax.fori_loop(0, 5, block, 0)
        for k, yk, peer in ((1, y1, ny1), (2, y2, ny2), (3, y3, ny3)):
            if k == 1:
                parts = (("a", yk, 0), ("b", 4 + yk, 1), ("c", 8 + yk, 2))
            else:
                parts = (("a", 4 + yk, 0), ("b", yk + 8 * h, 1))
            for tag, index, slot in parts:
                send(f"p{k}{tag}", PS.at[shard(index), :],
                     PR.at[pl.ds((k * 3 + slot) * arows, arows), :], peer)

    def part(buf, index):
        rows = shard(index)
        return (
            buf[rows, pl.ds(width, 128)].astype(F32),
            [buf[rows, pl.ds(hh * HDIM, HDIM)].astype(F32) for hh in range(heads)],
        )

    def put(index, state):
        rows = shard(index)
        peaks, sums, accs = state
        stats = []
        for hh in range(heads):
            SX[rows, pl.ds(hh * HDIM, HDIM)] = accs[hh].astype(BF)
            stats += [peaks[hh], sums[hh]]
        SX[rows, pl.ds(width, 128)] = pack_stats(stats, arows)

    def a5():
        got("p1a", "p1b", "p1c", "p2a", "p2b", "p3a", "p3b")
        put(1 - h, merge([part(PS, y + 8 * (1 - h)), part(PR, 3 + 2 * (1 - h)),
                          part(PR, 7), part(PR, 10)], heads))
        put(h, merge([part(PS, y + 8 * h), part(PR, 3 + 2 * h)], heads))
        send("pup", SX.at[pl.ds(arows, arows), :], RX.at[pl.ds(0, arows), :], nup)
        send("pdn", SX.at[pl.ds(0, arows), :], RX.at[pl.ds(arows, arows), :], ndn)

    def a6():
        got("pup", "pdn")
        _, sums, accs = merge(
            [part(PS, 4 + y), part(PR, 4), part(PR, 6), part(PR, 9), part(RX, 0), part(RX, 1)], heads
        )
        for hh in range(heads):
            ATTA[:, pl.ds(pl.multiple_of(c * width + hh * HDIM, HDIM), HDIM)] = (
                accs[hh] / sums[hh]
            ).astype(BF)
        mine = cols(c, width)
        send("ata", ATTA.at[:, mine], ATTA.at[:, mine], nc)

    got("xaz")
    send("xaf", XA.at[:, zcols], XA.at[:, zcols], nc)
    spread_on("k", KW)
    local["xa"].wait()
    local["wqa"].wait()
    got("xac", "xaf")
    QW[own] = dot(XA[...], WQA[...]).astype(BF)
    spread_x("q", QW)
    for i in range(1, 4):
        send_x(i)
    spread_y("q", QW)
    v1(0)
    wring1()
    spread_on("q", QW)
    local["x"].wait()
    local["wq"].wait()
    got("xc")
    spread_end("k")
    v2(0)
    v1(1)
    wring2()
    spread_end("q")
    a4()
    v2(1)
    v1(2)
    v3(0)
    v2(2)
    a5()
    v1(3)
    v3(1)
    v2(3)
    a6()
    v3(2)
    for name in ("wa0", "wa1"):
        local[name].wait()
        got(name)
    got("ata")
    att = ATTA[...]
    SBA[...] = dot(att, WOAC[:, feat:]).astype(BF)
    send("oza", SBA, RBA, nz)
    OWNA[...] = dot(att, WOAC[:, :feat])
    local["wo"].wait()
    got("woc", "wr2", "wl2")
    v3(3)
    for i in range(4):
        v4(i)
    got("oza")
    outa[...] = (OWNA[...] + RBA[...].astype(F32)).astype(BF)
    assert len(sent) == COPIES
    for copy in sent.values():
        copy.wait_send()


def finish(video, audio, outv, outa):
    outv[...] = video[...]
    outa[...] = audio[...]


def per_device(
    video_x, audio_x, video_kv, audio_kv, wq_video, wo_video, wq_audio, wo_audio,
    block_list, video_len, audio_len,
):
    vrows, feat = video_x.shape
    arows = audio_x.shape[0]
    full, width = wq_video.shape
    any_spec = pl.BlockSpec(memory_space=pl.ANY)
    smem = pl.BlockSpec(memory_space=pltpu.SMEM)
    vmem = pl.BlockSpec(memory_space=pltpu.VMEM)

    def V(*shape, dtype=BF):
        return pltpu.VMEM(shape, dtype)

    outs = pl.pallas_call(
        kernel,
        out_shape=[
            jax.ShapeDtypeStruct((vrows, feat), BF),
            jax.ShapeDtypeStruct((arows, feat), BF),
        ],
        in_specs=[any_spec] * 8 + [smem] * 3,
        out_specs=[vmem] * 2,
        scratch_shapes=[
            V(vrows, full), V(arows, full),
            V(vrows, 2, width), V(vrows, 2 * width), V(arows, 2, width),
            V(12, arows, 2 * width), V(12, arows, width),
            V(full, width), V(full, width), V(4 * width, feat), V(2 * width, 2 * feat),
            V(vrows, 4 * width), V(arows, 2 * width),
            V(arows, feat), V(arows, feat), V(arows, feat, dtype=F32),
            V(12 * arows, width + 128), V(12 * arows, width + 128),
            V(2 * arows, width + 128), V(2 * arows, width + 128),
            V(3 * BLOCK, 2 * width),
            pltpu.SemaphoreType.DMA((9,)),
            pltpu.SemaphoreType.DMA((COPIES,)),
            pltpu.SemaphoreType.DMA((COPIES,)),
        ],
        compiler_params=pltpu.CompilerParams(
            collective_id=0, has_side_effects=True, vmem_limit_bytes=56 * 2**20
        ),
        cost_estimate=pl.CostEstimate(
            flops=4_000_000_000, bytes_accessed=14_000_000, transcendentals=2_000_000
        ),
        name="twin_tower",
    )(
        video_x, audio_x, video_kv, audio_kv, wq_video, wo_video, wq_audio, wo_audio,
        block_list.T, video_len, audio_len,
    )
    return pl.pallas_call(
        finish,
        out_shape=[jax.ShapeDtypeStruct(o.shape, o.dtype) for o in outs],
        in_specs=[vmem] * 2,
        out_specs=[vmem] * 2,
        name="finish",
    )(*outs)


def solution(mesh):
    in_specs = (
        P("vid", "tp"), P("vid", "tp"), P("vid", None, "tp"), P("vid", None, "tp"),
        P(None, "tp"), P("tp", None), P(None, "tp"), P("tp", None), P(), P(), P(),
    )
    return jax.shard_map(
        per_device, mesh=mesh, in_specs=in_specs, out_specs=(P("vid", "tp"), P("vid", "tp")),
        check_vma=False,
    )
```

time: 561 us -> 65.9 us (0.12)
  waiting for transfers between devices: 383 us -> 0 us
  starting transfers between devices: 102 us -> 0 us
  Pallas kernels: 0 us -> 63.8 us
  local copies, waits for them, and re-layouts: 23.6 us -> 0 us
  matrix products: 21.8 us -> 0 us
  between operations: 15.5 us -> 1.93 us
  blocking collectives: 9.01 us -> 0 us
    ppermute x20 -> x0, waiting for transfers between devices: 204 us -> none  [shifted(): return lax.ppermute(array, axis, pairs)]
    reduce_scatter x2 -> x0, waiting for transfers between devices: 180 us -> none  [the longest x1 137 us: per_device(): lax.psum_scatter(audio_part.astype(jnp.bfloat16), 'tp', scatter_dimension...]
    ppermute x20 -> x0, starting transfers between devices: 101 us -> none  [shifted(): return lax.ppermute(array, axis, pairs)]
    pallas_call x0 -> x2, Pallas kernels: none -> 63.8 us  [the longest x1 61.7 us: per_device(): pl.pallas_call(kernel, out_shape=[jax.ShapeDtypeStruct((vrows, feat), BF)...]
    dot_general x7 -> x0, matrix products: 16.8 us -> none  [the longest x1 4.79 us: per_device(): jnp.dot(video_full, wq_video, preferred_element_type=jnp.float32)]
    unnamed x37 -> x0, local copies, waits for them, and re-layouts: 12.1 us -> none
    slice x4 -> x0, local copies, waits for them, and re-layouts: 10.6 us -> none  [the longest x2 6.85 us: fold_keys(): key_rows = shard_rows[:, 0].reshape(count, head_count, HDIM)]
    all_gather x1 -> x0, blocking collectives: 9.01 us -> none  [per_device(): lax.all_gather(audio_x, 'tp', axis=1, tiled=True)]
  transfers between devices with their start and end apart: 23 -> 0, of which waited for: 15 -> 0; matrix products, arithmetic and copies ran while one was open for 8% -> 0% of each run, Pallas kernels for 0% -> 0%
where the time goes in v1:
time: 65.9 us; the launch traced here: 65.7 us
  Pallas kernels  63.8 us (97%)
  between operations  1.93 us (3%)
    pallas_call x1, Pallas kernels, per_device(): pl.pallas_call(kernel, out_shape=[jax.ShapeDtypeStruct((vrows, feat), BF)...  61.7 us
    pallas_call x1, Pallas kernels, per_device(): pl.pallas_call(finish, out_shape=[jax.ShapeDtypeStruct(o.shape, o.dtype)...  2.09 us

profile of v1, /device:TPU:1, one launch (start us, length us, event | category | flops | bytes accessed | tf_op | source)
XLA Modules:
  0.0 65.7 jit_solution(2259016342135844835)
XLA Ops:
  1.9 61.7 %twin_tower.1 = (bf16[512,768]{1,0:T(8,128)(2,1)}, bf16[64,768]{1,0:T(8,128)(2,1)}) custom-call(bf16[512,768]{1,0:T(8,128)(2,1)} %x_hbm.1, bf16[64,768]{1,0:T(8,128)(2,1)} %xa_hbm.1, bf16[512,2,384]{2,1,0:T(2,128)(2,1)} %kv_hbm.1, bf16[64,2,384]{2,1,0:T(2,128)(2,1)} %akv_hbm.1, bf16[3072,384]{1,0:T(8,128)(2,1)} %wq_hbm.1, bf16[384,3072]{1,0:T(8,128)(2,1)} %wo_hbm.1, ...), custom_call_target="tpu_custom_call" | custom-call | flops 4000000000 | bytes 14000000 | tf_op jit(solution)/shard_map/twin_tower/pallas_call | solution.py:401
  63.6 2.1 %finish.1 = (bf16[512,768]{1,0:T(8,128)(2,1)}, bf16[64,768]{1,0:T(8,128)(2,1)}) custom-call(bf16[512,768]{1,0:T(8,128)(2,1)} %get-tuple-element.4.video, bf16[64,768]{1,0:T(8,128)(2,1)} %get-tuple-element.5.audio), custom_call_target="tpu_custom_call" | custom-call | tf_op jit(solution)/shard_map/finish/pallas_call | solution.py:434

commit v2 on v1

--- a/solution.py
+++ b/solution.py
@@ -68,10 +68,10 @@
 
 
 def kernel(
-    x_hbm, xa_hbm, kv_hbm, akv_hbm, wq_hbm, wo_hbm, wqa_hbm, woa_hbm, bl, vlen, alen,
+    x_hbm, xa_hbm, kv_hbm, akv_hbm, wq_hbm, wo_hbm, wqa_hbm, woa_hbm, bl_hbm, vlen_hbm, alen_hbm,
     outv, outa,
     X, XA, kvraw, VK, akraw, KW, QW, WQ, WQA, WOC, WOAC, ATT, ATTA,
-    SBA, RBA, OWNA, PS, PR, SX, RX, KS, lsem, ssem, rsem,
+    SBA, RBA, OWNA, PS, PR, SX, RX, KS, bl, vlen, alen, lsem, ssem, rsem,
 ):
     width = WQ.shape[1]
     heads = width // HDIM
@@ -110,6 +110,9 @@
         return pl.ds(pl.multiple_of(i * arows, arows), arows)
 
     load("ak", 0, akv_hbm, akraw)
+    load("bl", 9, bl_hbm, bl)
+    load("vlen", 10, vlen_hbm, vlen)
+    load("alen", 11, alen_hbm, alen)
     load("xa", 1, xa_hbm, XA.at[:, cols(t, feat)])
     load("x", 2, x_hbm, X.at[:, cols(t, feat)])
     load("wqa", 3, wqa_hbm, WQA)
@@ -168,9 +171,9 @@
     def spread_end(p):
         got(*(p + s for s in ("y1", "y2", "y3", "f1a", "f1b", "f2", "f3")))
 
-    spread_x("k", KW)
     send("xaz", xa_hbm, XA.at[:, tcols], nz)
     send("xac", xa_hbm, XA.at[:, tcols], nc)
+    spread_x("k", KW)
     send_x(0)
     spread_y("k", KW)
     send("xc", x_hbm, X.at[:, tcols], nc)
@@ -257,7 +260,7 @@
     def a4():
         base = v * 4
 
-        def block(j, _):
+        def block(j):
             g = h + j
             blk = 2 * row - 2 + g
             bias = []
@@ -278,17 +281,22 @@
                 stats += [m, jnp.sum(e, axis=1, keepdims=True)]
                 PS[rows, hc] = dot(e.astype(BF), VK[:, pl.ds(width + hh * HDIM, HDIM)]).astype(BF)
             PS[rows, pl.ds(width, 128)] = pack_stats(stats, BLOCK)
-            return 0
-
-        lax.fori_loop(0, 5, block, 0)
-        for k, yk, peer in ((1, y1, ny1), (2, y2, ny2), (3, y3, ny3)):
-            if k == 1:
-                parts = (("a", yk, 0), ("b", 4 + yk, 1), ("c", 8 + yk, 2))
-            else:
-                parts = (("a", 4 + yk, 0), ("b", yk + 8 * h, 1))
-            for tag, index, slot in parts:
-                send(f"p{k}{tag}", PS.at[shard(index), :],
-                     PR.at[pl.ds((k * 3 + slot) * arows, arows), :], peer)
+
+        def give(name, index, slot, peer):
+            send(name, PS.at[shard(index), :], PR.at[pl.ds(slot * arows, arows), :], peer)
+
+        for j in (1, 3):
+            block(j)
+        give("p2a", 4 + y2, 6, ny2)
+        give("p3a", 4 + y3, 9, ny3)
+        give("p2b", y2 + 8 * h, 7, ny2)
+        give("p3b", y3 + 8 * h, 10, ny3)
+        block(0)
+        give("p1a", y1, 3, ny1)
+        block(4)
+        give("p1c", 8 + y1, 5, ny1)
+        block(2)
+        give("p1b", 4 + y1, 4, ny1)
 
     def part(buf, index):
         rows = shard(index)
@@ -326,39 +334,41 @@
         mine = cols(c, width)
         send("ata", ATTA.at[:, mine], ATTA.at[:, mine], nc)
 
+    for name in ("bl", "vlen", "alen"):
+        local[name].wait()
     got("xaz")
     send("xaf", XA.at[:, zcols], XA.at[:, zcols], nc)
-    spread_on("k", KW)
     local["xa"].wait()
     local["wqa"].wait()
     got("xac", "xaf")
     QW[own] = dot(XA[...], WQA[...]).astype(BF)
     spread_x("q", QW)
-    for i in range(1, 4):
-        send_x(i)
+    send_x(1)
     spread_y("q", QW)
+    spread_on("q", QW)
+    send_x(2)
+    send_x(3)
+    spread_on("k", KW)
+    wring1()
     v1(0)
-    wring1()
-    spread_on("q", QW)
+    spread_end("q")
+    a4()
+    v1(1)
+    wring2()
     local["x"].wait()
     local["wq"].wait()
     got("xc")
     spread_end("k")
     v2(0)
-    v1(1)
-    wring2()
-    spread_end("q")
-    a4()
+    v1(2)
+    a5()
     v2(1)
-    v1(2)
     v3(0)
     v2(2)
-    a5()
     v1(3)
+    a6()
     v3(1)
     v2(3)
-    a6()
-    v3(2)
     for name in ("wa0", "wa1"):
         local[name].wait()
         got(name)
@@ -369,8 +379,10 @@
     OWNA[...] = dot(att, WOAC[:, :feat])
     local["wo"].wait()
     got("woc", "wr2", "wl2")
+    v3(2)
+    v4(0)
     v3(3)
-    for i in range(4):
+    for i in range(1, 4):
         v4(i)
     got("oza")
     outa[...] = (OWNA[...] + RBA[...].astype(F32)).astype(BF)
@@ -392,7 +404,6 @@
     arows = audio_x.shape[0]
     full, width = wq_video.shape
     any_spec = pl.BlockSpec(memory_space=pl.ANY)
-    smem = pl.BlockSpec(memory_space=pltpu.SMEM)
     vmem = pl.BlockSpec(memory_space=pltpu.VMEM)
 
     def V(*shape, dtype=BF):
@@ -404,7 +415,7 @@
             jax.ShapeDtypeStruct((vrows, feat), BF),
             jax.ShapeDtypeStruct((arows, feat), BF),
         ],
-        in_specs=[any_spec] * 8 + [smem] * 3,
+        in_specs=[any_spec] * 11,
         out_specs=[vmem] * 2,
         scratch_shapes=[
             V(vrows, full), V(arows, full),
@@ -416,7 +427,8 @@
             V(12 * arows, width + 128), V(12 * arows, width + 128),
             V(2 * arows, width + 128), V(2 * arows, width + 128),
             V(3 * BLOCK, 2 * width),
-            pltpu.SemaphoreType.DMA((9,)),
+            pltpu.SMEM(block_list.shape[::-1], jnp.int32), pltpu.SMEM((1,), jnp.int32), pltpu.SMEM((1,), jnp.int32),
+            pltpu.SemaphoreType.DMA((12,)),
             pltpu.SemaphoreType.DMA((COPIES,)),
             pltpu.SemaphoreType.DMA((COPIES,)),
         ],

time: 65.9 us -> 63.2 us (0.959)
  Pallas kernels: 63.8 us -> 60.8 us
    pallas_call x1, Pallas kernels: 61.7 us -> 58.7 us  [per_device(): pl.pallas_call(kernel, out_shape=[jax.ShapeDtypeStruct((vrows, feat), BF)...]
where the time goes in v2:
time: 63.2 us; the launch traced here: 62.7 us
  Pallas kernels  60.8 us (96%)
  between operations  1.93 us (3%)
    pallas_call x1, Pallas kernels, per_device(): pl.pallas_call(kernel, out_shape=[jax.ShapeDtypeStruct((vrows, feat), BF)...  58.7 us
    pallas_call x1, Pallas kernels, per_device(): pl.pallas_call(finish, out_shape=[jax.ShapeDtypeStruct(o.shape, o.dtype)...  2.09 us

profile of v2, /device:TPU:1, one launch (start us, length us, event | category | flops | bytes accessed | tf_op | source)
XLA Modules:
  0.0 62.7 jit_solution(9432742822744701516)
XLA Ops:
  1.9 58.7 %twin_tower.1 = (bf16[512,768]{1,0:T(8,128)(2,1)}, bf16[64,768]{1,0:T(8,128)(2,1)}) custom-call(bf16[512,768]{1,0:T(8,128)(2,1)} %x_hbm.1, bf16[64,768]{1,0:T(8,128)(2,1)} %xa_hbm.1, bf16[512,2,384]{2,1,0:T(2,128)(2,1)} %kv_hbm.1, bf16[64,2,384]{2,1,0:T(2,128)(2,1)} %akv_hbm.1, bf16[3072,384]{1,0:T(8,128)(2,1)} %wq_hbm.1, bf16[384,3072]{1,0:T(8,128)(2,1)} %wo_hbm.1, ...), custom_call_target="tpu_custom_call" | custom-call | flops 4000000000 | bytes 14000000 | tf_op jit(solution)/shard_map/twin_tower/pallas_call | solution.py:412
  60.6 2.1 %finish.1 = (bf16[512,768]{1,0:T(8,128)(2,1)}, bf16[64,768]{1,0:T(8,128)(2,1)}) custom-call(bf16[512,768]{1,0:T(8,128)(2,1)} %get-tuple-element.4.video, bf16[64,768]{1,0:T(8,128)(2,1)} %get-tuple-element.5.audio), custom_call_target="tpu_custom_call" | custom-call | tf_op jit(solution)/shard_map/finish/pallas_call | solution.py:446

commit v3 on v2

--- a/solution.py
+++ b/solution.py
@@ -338,37 +338,37 @@
         local[name].wait()
     got("xaz")
     send("xaf", XA.at[:, zcols], XA.at[:, zcols], nc)
+    spread_on("k", KW)
     local["xa"].wait()
     local["wqa"].wait()
     got("xac", "xaf")
     QW[own] = dot(XA[...], WQA[...]).astype(BF)
     spread_x("q", QW)
+    spread_y("q", QW)
     send_x(1)
-    spread_y("q", QW)
     spread_on("q", QW)
     send_x(2)
     send_x(3)
-    spread_on("k", KW)
+    v1(0)
     wring1()
-    v1(0)
-    spread_end("q")
-    a4()
-    v1(1)
-    wring2()
     local["x"].wait()
     local["wq"].wait()
     got("xc")
     spread_end("k")
     v2(0)
+    spread_end("q")
+    a4()
+    v1(1)
+    wring2()
     v1(2)
+    v2(1)
     a5()
-    v2(1)
     v3(0)
     v2(2)
     v1(3)
-    a6()
     v3(1)
     v2(3)
+    a6()
     for name in ("wa0", "wa1"):
         local[name].wait()
         got(name)

time: 63.2 us -> 59.5 us (0.941)
  Pallas kernels: 60.8 us -> 57.4 us
    pallas_call x1, Pallas kernels: 58.7 us -> 55.4 us  [per_device(): pl.pallas_call(kernel, out_shape=[jax.ShapeDtypeStruct((vrows, feat), BF)...]
where the time goes in v3:
time: 59.5 us; the launch traced here: 59.4 us
  Pallas kernels  57.4 us (96%)
  between operations  1.93 us (3%)
    pallas_call x1, Pallas kernels, per_device(): pl.pallas_call(kernel, out_shape=[jax.ShapeDtypeStruct((vrows, feat), BF)...  55.4 us
    pallas_call x1, Pallas kernels, per_device(): pl.pallas_call(finish, out_shape=[jax.ShapeDtypeStruct(o.shape, o.dtype)...  2.09 us

profile of v3, /device:TPU:1, one launch (start us, length us, event | category | flops | bytes accessed | tf_op | source)
XLA Modules:
  0.0 59.4 jit_solution(17681590744420125101)
XLA Ops:
  1.9 55.4 %twin_tower.1 = (bf16[512,768]{1,0:T(8,128)(2,1)}, bf16[64,768]{1,0:T(8,128)(2,1)}) custom-call(bf16[512,768]{1,0:T(8,128)(2,1)} %x_hbm.1, bf16[64,768]{1,0:T(8,128)(2,1)} %xa_hbm.1, bf16[512,2,384]{2,1,0:T(2,128)(2,1)} %kv_hbm.1, bf16[64,2,384]{2,1,0:T(2,128)(2,1)} %akv_hbm.1, bf16[3072,384]{1,0:T(8,128)(2,1)} %wq_hbm.1, bf16[384,3072]{1,0:T(8,128)(2,1)} %wo_hbm.1, ...), custom_call_target="tpu_custom_call" | custom-call | flops 4000000000 | bytes 14000000 | tf_op jit(solution)/shard_map/twin_tower/pallas_call | solution.py:412
  57.3 2.1 %finish.1 = (bf16[512,768]{1,0:T(8,128)(2,1)}, bf16[64,768]{1,0:T(8,128)(2,1)}) custom-call(bf16[512,768]{1,0:T(8,128)(2,1)} %get-tuple-element.4.video, bf16[64,768]{1,0:T(8,128)(2,1)} %get-tuple-element.5.audio), custom_call_target="tpu_custom_call" | custom-call | tf_op jit(solution)/shard_map/finish/pallas_call | solution.py:446

commit v4 on v3

--- a/solution.py
+++ b/solution.py
@@ -372,6 +372,7 @@
     for name in ("wa0", "wa1"):
         local[name].wait()
         got(name)
+    v3(2)
     got("ata")
     att = ATTA[...]
     SBA[...] = dot(att, WOAC[:, feat:]).astype(BF)
@@ -379,7 +380,6 @@
     OWNA[...] = dot(att, WOAC[:, :feat])
     local["wo"].wait()
     got("woc", "wr2", "wl2")
-    v3(2)
     v4(0)
     v3(3)
     for i in range(1, 4):
@@ -391,9 +391,24 @@
         copy.wait_send()
 
 
-def finish(video, audio, outv, outa):
-    outv[...] = video[...]
-    outa[...] = audio[...]
+def finish(video, audio, outv, outa, bufv, bufa, sem_in, sem_out):
+    rows = video.shape[0] // 4
+    parts = [(video, bufv, outv, pl.ds(i * rows, rows)) for i in range(4)]
+    parts.append((audio, bufa, outa, pl.ds(0, audio.shape[0])))
+    copies = [
+        (
+            pltpu.make_async_copy(src.at[at], buf.at[at], sem_in.at[i]),
+            pltpu.make_async_copy(buf.at[at], dst.at[at], sem_out.at[i]),
+        )
+        for i, (src, buf, dst, at) in enumerate(parts)
+    ]
+    for first, _ in copies:
+        first.start()
+    for first, second in copies:
+        first.wait()
+        second.start()
+    for _, second in copies:
+        second.wait()
 
 
 def per_device(
@@ -446,8 +461,12 @@
     return pl.pallas_call(
         finish,
         out_shape=[jax.ShapeDtypeStruct(o.shape, o.dtype) for o in outs],
-        in_specs=[vmem] * 2,
-        out_specs=[vmem] * 2,
+        in_specs=[any_spec] * 2,
+        out_specs=[any_spec] * 2,
+        scratch_shapes=[
+            V(vrows, feat), V(arows, feat),
+            pltpu.SemaphoreType.DMA((5,)), pltpu.SemaphoreType.DMA((5,)),
+        ],
         name="finish",
     )(*outs)
 

time: 59.5 us -> 59.4 us (level)
  no operation moved by 1% of the time
where the time goes in v4:
time: 59.4 us; the launch traced here: 59.3 us
  Pallas kernels  57.4 us (97%)
  between operations  1.93 us (3%)
    pallas_call x1, Pallas kernels, per_device(): pl.pallas_call(kernel, out_shape=[jax.ShapeDtypeStruct((vrows, feat), BF)...  55.3 us
    pallas_call x1, Pallas kernels, per_device(): pl.pallas_call(finish, out_shape=[jax.ShapeDtypeStruct(o.shape, o.dtype)...  2.01 us

profile of v4, /device:TPU:1, one launch (start us, length us, event | category | flops | bytes accessed | tf_op | source)
XLA Modules:
  0.0 59.3 jit_solution(17466975013899951557)
XLA Ops:
  1.9 55.3 %twin_tower.1 = (bf16[512,768]{1,0:T(8,128)(2,1)}, bf16[64,768]{1,0:T(8,128)(2,1)}) custom-call(bf16[512,768]{1,0:T(8,128)(2,1)} %x_hbm.1, bf16[64,768]{1,0:T(8,128)(2,1)} %xa_hbm.1, bf16[512,2,384]{2,1,0:T(2,128)(2,1)} %kv_hbm.1, bf16[64,2,384]{2,1,0:T(2,128)(2,1)} %akv_hbm.1, bf16[3072,384]{1,0:T(8,128)(2,1)} %wq_hbm.1, bf16[384,3072]{1,0:T(8,128)(2,1)} %wo_hbm.1, ...), custom_call_target="tpu_custom_call" | custom-call | flops 4000000000 | bytes 14000000 | tf_op jit(solution)/shard_map/twin_tower/pallas_call | solution.py:427
  57.3 2.0 %finish.1 = (bf16[512,768]{1,0:T(8,128)(2,1)}, bf16[64,768]{1,0:T(8,128)(2,1)}) custom-call(bf16[512,768]{1,0:T(8,128)(2,1)} %get-tuple-element.4.video, bf16[64,768]{1,0:T(8,128)(2,1)} %get-tuple-element.5.audio), custom_call_target="tpu_custom_call" | custom-call | tf_op jit(solution)/shard_map/finish/pallas_call | solution.py:461
